TPU v7x, 32 devices: a whole 2x2x4 slice. The times are simulated.
32 devices in a mesh: row: 4 (over z), col: 4 (over y, x), depth: 2 (over core).
Axes of the slice: x: 2, y: 2, z: 4, core: 2. Of those that a mesh axis runs over, the one named last changes fastest.
Arguments:
- a_blocks: bfloat16 [4, 2, 2, 4, 128, 128], P('row', 'depth', None, 'col'), may hold values from -6 to 6
- a_index: int32 [4, 2, 2, 4], P('row', 'depth', None, 'col'), may hold values from 0 to 31, as said below
- a_count: int32 [4, 2, 2], P('row'), may hold values from 1 to 4
- b_blocks: bfloat16 [4, 2, 2, 4, 128, 128], P('col', 'depth', None, 'row'), may hold values from -0.25 to 0.25
- b_index: int32 [4, 2, 2, 4], P('col', 'depth', None, 'row'), may hold values from 0 to 63, as said below
- b_count: int32 [4, 2, 2], P('col'), may hold values from 1 to 4
- c_mask: int32 [16, 32], P('row', ('col', 'depth')), may hold values 0 or 1
Outputs:
- c_matrix: bfloat16 [2048, 4096], P('row', ('col', 'depth'))
Inputs may be any that keep to these rules, and one draw needn't show every extreme that they name: `a_index`: within each list the positions of all slots are distinct. `b_index`: within each list the positions of all slots are distinct.
All inputs are finite; a program needn't handle non-finite values. No bound on the sum of `c_mask` on one device may be relied on, other than what follows from the above.
Results may differ from a plain program's by a relative error of at most 0.0049.
Values may be sent and summed in bfloat16 or wider, within the bound.
A program may use at most 64 MiB of HBM per device.

v0:
```python
import jax
import jax.numpy as jnp
from jax import lax
from jax.sharding import PartitionSpec as P

BS = 128
PW = 8
STEPS = 2
RB = 4
CB = 8


def panel_term(a_blk, a_idx, a_cnt, b_blk, b_idx, b_cnt, col_start, col_count):
    a_slots = a_idx.shape[0]
    b_slots = b_idx.shape[0]
    live_a = jnp.arange(a_slots, dtype=jnp.int32) < a_cnt
    onehot_a = (
        (a_idx[:, None] == jnp.arange(RB * PW, dtype=jnp.int32)[None, :]) & live_a[:, None]
    ).astype(jnp.bfloat16)
    dense = jnp.einsum("sp,sxy->pxy", onehot_a, a_blk, preferred_element_type=jnp.float32).astype(
        jnp.bfloat16
    )
    stacked = dense.reshape(RB, PW, BS, BS).transpose(0, 2, 1, 3).reshape(RB * BS, PW, BS)
    inner_b = b_idx // CB
    column_b = b_idx % CB
    live_b = jnp.arange(b_slots, dtype=jnp.int32) < b_cnt
    picker = (inner_b[:, None] == jnp.arange(PW, dtype=jnp.int32)[None, :]).astype(jnp.bfloat16)
    columns = jnp.einsum("sj,mjk->smk", picker, stacked, preferred_element_type=jnp.float32).astype(
        jnp.bfloat16
    )
    products = jnp.einsum("smk,skl->sml", columns, b_blk, preferred_element_type=jnp.float32)
    placer = (
        (column_b[:, None] - col_start == jnp.arange(col_count, dtype=jnp.int32)[None, :])
        & live_b[:, None]
    ).astype(jnp.float32)
    placed = jnp.einsum(
        "sn,sml->mnl",
        placer,
        products,
        precision=lax.Precision.HIGHEST,
        preferred_element_type=jnp.float32,
    )
    return placed.reshape(RB * BS, col_count * BS)


def apply_mask(total, c_mask):
    half = c_mask.shape[1]
    kept = total.reshape(RB, BS, half, BS) * c_mask.astype(jnp.float32)[:, None, :, None]
    return kept.reshape(RB * BS, half * BS).astype(jnp.bfloat16)


def local(a_blocks, a_index, a_count, b_blocks, b_index, b_count, c_mask):
    group = lax.axis_index("depth")
    total = jnp.zeros((RB * BS, CB * BS), jnp.float32)
    for step in range(STEPS):
        got_a, got_ai = (
            lax.all_gather(a_blocks[:, :, step : step + 1], "col", axis=3, tiled=True),
            lax.all_gather(a_index[:, :, step : step + 1], "col", axis=3, tiled=True),
        )
        got_b, got_bi = (
            lax.all_gather(b_blocks[:, :, step : step + 1], "row", axis=3, tiled=True),
            lax.all_gather(b_index[:, :, step : step + 1], "row", axis=3, tiled=True),
        )
        total = total + panel_term(
            got_a[0, 0, 0],
            got_ai[0, 0, 0],
            a_count[0, group, step],
            got_b[0, 0, 0],
            got_bi[0, 0, 0],
            b_count[0, group, step],
            0,
            CB,
        )
    summed = lax.psum_scatter(
        total.astype(jnp.bfloat16), "depth", scatter_dimension=1, tiled=True
    ).astype(jnp.float32)
    return apply_mask(summed, c_mask)


def solution(mesh):
    in_specs = (
        P("row", "depth", None, "col", None, None),
        P("row", "depth", None, "col"),
        P("row", None, None),
        P("col", "depth", None, "row", None, None),
        P("col", "depth", None, "row"),
        P("col", None, None),
        P("row", ("col", "depth")),
    )
    out_specs = P("row", ("col", "depth"))
    return jax.shard_map(local, mesh=mesh, in_specs=in_specs, out_specs=out_specs, check_vma=False)
```

profile of v0, /device:TPU:0, one launch (start us, length us, event | category | flops | bytes accessed | tf_op | source)
XLA Modules:
  0.0 105.9 jit_solution(16245036767624238617)
XLA Ops:
  6.5 0.0 copy-start
  6.5 0.0 reduce-scatter.2.cloned.1.call-start
  6.5 1.4 %constant_dynamic-slice_fusion = (s32[1,1,1]{2,1,0:T(1,128)}, s32[1,1,1]{2,1,0:T(1,128)}, s32[1,1,1]{2,1,0:T(1,128)}, s32[1,1,1]{2,1,0:T(1,128)}) fusion(s32[1,2,2]{2,1,0:T(2,128)} %param.12, s32[]{:T(128)S(6)} %select_n.42, s32[1,2,2]{2,1,0:T(2,128)} %param.9), kind=kLoop, calls=%fused_computation.55 | loop fusion | bytes 36 | tf_op jit(solution)/shard_map/dynamic_slice | solution.py:70
  7.9 0.6 iota_compare_fusion.9
  8.6 1.4 %fusion.45 = (s32[1,1,1,1]{2,3,1,0:T(1,128)}, s32[1,1,1,1]{2,3,1,0:T(1,128)}) fusion(s32[1,1,2,1]{2,3,1,0:T(1,128)} %param.8), kind=kLoop, calls=%fused_computation.74 | loop fusion | bytes 16 | tf_op jit(solution)/shard_map/slice | solution.py:58
  9.9 0.8 fusion.43
  10.7 9.9 %all_gather.26 = bf16[1,1,1,4,128,128]{5,4,2,1,0,3:T(8,128)(2,1)S(1)} all-gather(bf16[1,1,1,1,128,128]{5,4,2,1,0,3:T(8,128)(2,1)S(1)} %get-tuple-element.12), channel_id=1, replica_groups=mesh['row'=4,'col'=4,'depth'=2] {'col'}, dimensions={3}, use_global_device_ids=true | all-gather | bytes 163840 | tf_op jit(solution)/shard_map/all_gather | solution.py:57
  20.6 1.3 %fusion.44 = (s32[1,1,1,1]{2,3,1,0:T(1,128)}, s32[1,1,1,1]{2,3,1,0:T(1,128)}) fusion(s32[1,1,2,1]{2,3,1,0:T(1,128)} %param.11), kind=kLoop, calls=%fused_computation.73 | loop fusion | bytes 16 | tf_op jit(solution)/shard_map/slice | solution.py:62
  22.0 1.2 %dynamic-slice.1 = u32[1]{0:T(128)} dynamic-slice(u32[32]{0:T(128)} %constant.62, u32[]{:T(128)S(6)} %add.45), dynamic_slice_sizes={1} | dynamic-slice | bytes 12
  23.2 1.4 %bitcast_dynamic-update-slice_fusion = s32[4]{0:T(128)S(1)} fusion(s32[4]{0:T(128)S(1)} %broadcast.135.clone.1, u32[]{:T(128)} %bitcast.4, s32[1,1,1,1]{2,3,1,0:T(1,128)} %get-tuple-element.23), kind=kLoop, calls=%fused_computation.63 | loop fusion | bytes 24
  24.6 1.3 %bitcast_dynamic-update-slice_fusion.2 = s32[4]{0:T(128)S(1)} fusion(s32[4]{0:T(128)S(1)} %broadcast.135.clone, u32[]{:T(128)} %bitcast.4, s32[1,1,1,1]{2,3,1,0:T(1,128)} %get-tuple-element.24), kind=kLoop, calls=%fused_computation.65 | loop fusion | bytes 24
  25.9 1.2 %dynamic-slice = u32[1]{0:T(128)} dynamic-slice(u32[32]{0:T(128)} %constant.57, u32[]{:T(128)S(6)} %add.45), dynamic_slice_sizes={1} | dynamic-slice | bytes 12
  27.1 7.3 %all-reduce.4 = (s32[4]{0:T(128)S(1)}, s32[4]{0:T(128)S(1)}) all-reduce(s32[4]{0:T(128)S(1)} %bitcast_dynamic-update-slice_fusion.2, s32[4]{0:T(128)S(1)} %bitcast_dynamic-update-slice_fusion), channel_id=1, replica_groups=mesh['row'=4,'col'=4,'depth'=2] {'col'}, use_global_device_ids=true, to_apply=%add.1 | all-reduce | flops 8 | bytes 64
  34.5 1.3 %bitcast_dynamic-update-slice_fusion.1 = s32[4]{0:T(128)S(1)} fusion(s32[4]{0:T(128)S(1)} %broadcast.135.clone.3, u32[]{:T(128)} %bitcast.1, s32[1,1,1,1]{2,3,1,0:T(1,128)} %get-tuple-element.21), kind=kLoop, calls=%fused_computation.64 | loop fusion | bytes 24
  35.8 1.3 %bitcast_dynamic-update-slice_fusion.3 = s32[4]{0:T(128)S(1)} fusion(s32[4]{0:T(128)S(1)} %broadcast.135.clone.2, u32[]{:T(128)} %bitcast.1, s32[1,1,1,1]{2,3,1,0:T(1,128)} %get-tuple-element.22), kind=kLoop, calls=%fused_computation.66 | loop fusion | bytes 24
  37.1 0.6 fusion
  37.7 0.2 copy.16
  37.9 8.5 %all-reduce.5 = (s32[4]{0:T(128)S(1)}, s32[4]{0:T(128)S(1)}) all-reduce(s32[4]{0:T(128)S(1)} %bitcast_dynamic-update-slice_fusion.3, s32[4]{0:T(128)S(1)} %bitcast_dynamic-update-slice_fusion.1), channel_id=1, replica_groups=mesh['row'=4,'col'=4,'depth'=2] {'row'}, use_global_device_ids=true, to_apply=%add | all-reduce | flops 8 | bytes 64 | tf_op jit(solution)/shard_map/squeeze | solution.py:69
  46.4 0.0 copy-done
  46.4 13.3 %all_gather.27 = bf16[1,1,1,4,128,128]{5,4,2,1,0,3:T(8,128)(2,1)S(1)} all-gather(bf16[1,1,1,1,128,128]{5,4,2,1,0,3:T(8,128)(2,1)S(1)} %get-tuple-element.10), channel_id=1, replica_groups=mesh['row'=4,'col'=4,'depth'=2] {'row'}, dimensions={3}, use_global_device_ids=true | all-gather | bytes 163840 | tf_op jit(solution)/shard_map/all_gather | solution.py:61
  59.7 0.7 iota_compare_fusion.8
  60.4 0.6 iota_compare_fusion.7
  61.0 7.5 %all_gather.30 = bf16[1,1,1,4,128,128]{5,4,2,1,0,3:T(8,128)(2,1)S(1)} all-gather(bf16[1,1,1,1,128,128]{5,4,2,1,0,3:T(8,128)(2,1)S(1)} %get-tuple-element.11), channel_id=1, replica_groups=mesh['row'=4,'col'=4,'depth'=2] {'col'}, dimensions={3}, use_global_device_ids=true | all-gather | bytes 163840 | tf_op jit(solution)/shard_map/all_gather | solution.py:57
  68.5 0.6 fusion.1
  69.1 0.2 copy.22
  69.3 13.3 %all_gather.31 = bf16[1,1,1,4,128,128]{5,4,2,1,0,3:T(8,128)(2,1)S(1)} all-gather(bf16[1,1,1,1,128,128]{5,4,2,1,0,3:T(8,128)(2,1)S(1)} %get-tuple-element.9), channel_id=1, replica_groups=mesh['row'=4,'col'=4,'depth'=2] {'row'}, dimensions={3}, use_global_device_ids=true | all-gather | bytes 163840 | tf_op jit(solution)/shard_map/all_gather | solution.py:61
  82.6 0.6 iota_compare_fusion.6
  83.2 0.5 convolution_convert_fusion.3
  83.7 0.3 fusion.8
  84.0 0.5 convolution_convert_fusion.2
  84.5 0.3 fusion.6
  84.8 1.8 %fusion.4 = f32[512,128,8]{1,2,0:T(8,128)S(1)} fusion(f32[4,512,128]{2,1,0:T(8,128)S(1)} %fusion.8, s32[4]{0:T(128)S(1)} %get-tuple-element.19, pred[4]{0:T(512)(128)(4,1)S(1)} %iota_compare_fusion.8), kind=kOutput, calls=%fused_computation.11 | convolution fusion | flops 25165888 | bytes 3145748 | tf_op jit(solution)/shard_map/sn,sml->mnl/dot_general | solution.py:36
  86.5 1.9 %add_convert_fusion = bf16[512,128,8]{1,2,0:T(8,128)(2,1)S(1)} fusion(f32[512,128,8]{1,2,0:T(8,128)S(1)} %fusion.4, f32[4,512,128]{2,1,0:T(8,128)S(1)} %fusion.6, s32[4]{0:T(128)S(1)} %get-tuple-element.17, pred[4]{0:T(512)(128)(4,1)S(1)} %iota_compare_fusion.6), kind=kOutput, calls=%fused_computation | convolution fusion | flops 26214464 | bytes 4194324 | tf_op jit(solution)/shard_map/sn,sml->mnl/dot_general | solution.py:36
  88.5 0.0 copy-start.1
  88.5 1.3 %copy.46 = bf16[64,8,8,128]{3,1,2,0:T(8,128)(2,1)} copy(bf16[64,8,8,128]{3,2,1,0:T(8,128)(2,1)S(1)} %bitcast.71) | data formatting | bytes 2097152
  89.7 0.0 reduce-scatter.2.cloned.1.call-update
  89.7 0.0 copy-done.1
  89.8 7.0 %reduce-scatter.2.cloned.1.call-done = bf16[512,512]{1,0:T(8,128)(2,1)} async-done(((bf16[512,1024]{1,0:T(8,128)(2,1)}), bf16[512,512]{1,0:T(8,128)(2,1)}) %reduce-scatter.2.cloned.1.call-update) | async-done | bytes 524304 | tf_op jit(solution)/shard_map/reduce_scatter | solution.py:74
  96.8 0.2 mul.11
  97.0 2.0 %fusion.2 = bf16[512,512]{1,0:T(8,128)(2,1)} fusion(f32[64,8,4,128]{3,2,1,0:T(4,128)S(1)} %bitcast.75, bf16[512,512]{1,0:T(8,128)(2,1)} %reduce-scatter.2.cloned.1.call-done), kind=kLoop, calls=%fused_computation.8 | loop fusion | flops 786432 | bytes 2097152 | tf_op jit(solution)/shard_map/convert_element_type | solution.py:49
  (8 shorter events, 0.0 us)
Async XLA Ops:
  6.5 39.8 %copy-start = (bf16[1,1,2,1,128,128]{5,4,3,2,1,0:T(8,128)(2,1)S(1)}, bf16[1,1,2,1,128,128]{5,4,3,2,1,0:T(8,128)(2,1)}, u32[]{:S(2)}) copy-start(bf16[1,1,2,1,128,128]{5,4,3,2,1,0:T(8,128)(2,1)} %param.10) | copy-start | bytes 196612
  6.5 90.3 %reduce-scatter.2.cloned.1.call-start = ((), (), s32[]{:S(2)}) async-start(), calls=%async_computation.1 | async-start | bytes 1572864 | tf_op jit(solution)/shard_map/reduce_scatter | solution.py:74
  88.5 1.3 %copy-start.1 = (s32[4,4]{1,0:T(4,128)S(1)}, s32[4,4]{1,0:T(4,128)}, u32[]{:S(2)}) copy-start(s32[4,4]{1,0:T(4,128)} %param.13) | copy-start | bytes 196
Sparse Core Ops, SparseCore 0:
  89.9 6.8 reduce-scatter.1
where the time goes:
time: 106 us
  blocking collectives  59.9 us (57%)
  local copies, waits for them, and re-layouts  14.4 us (14%)
  between operations  13.6 us (13%)
  waiting for transfers between devices  7.06 us (7%)
  matrix products  6.35 us (6%)
  other arithmetic  4.52 us (4%)
    all_gather x2, blocking collectives, local(): lax.all_gather(b_blocks[:, :, step:step + 1], 'row', axis=3, tiled=True)  26.7 us
    all_gather x2, blocking collectives, local(): lax.all_gather(a_blocks[:, :, step:step + 1], 'col', axis=3, tiled=True)  17.4 us
    unnamed x15, local copies, waits for them, and re-layouts  9 us
    squeeze x1, blocking collectives, local(): got_bi[0, 0, 0]  8.48 us
    unnamed x1, blocking collectives  7.35 us
    reduce_scatter x1, waiting for transfers between devices, local(): lax.psum_scatter(total.astype(jnp.bfloat16), 'depth', scatter_dimension=1...  7.04 us
    dot_general x2, matrix products, panel_term(): jnp.einsum('sn,sml->mnl', placer, products, precision=lax.Precision.HIGHE...  3.67 us
  transfers between devices with their start and end apart: 1, of which 1 were waited for; matrix products, arithmetic and copies ran while one was open for 0% of the time, Pallas kernels for 0%

commit v1 on v0

--- a/solution.py
+++ b/solution.py
@@ -1,13 +1,228 @@
+import functools
+
 import jax
 import jax.numpy as jnp
 from jax import lax
+from jax.experimental import pallas as pl
+from jax.experimental.pallas import tpu as pltpu
 from jax.sharding import PartitionSpec as P
 
 BS = 128
 PW = 8
-STEPS = 2
 RB = 4
 CB = 8
+TAIL = 16
+BF = jnp.bfloat16
+F32 = jnp.float32
+
+
+def _rows(values):
+    row = lax.broadcasted_iota(jnp.int32, (TAIL, BS), 0)
+    tile = jnp.zeros((TAIL, BS), jnp.int32)
+    for r, value in enumerate(values):
+        tile = jnp.where(row == r, value, tile)
+    return tile.astype(F32).astype(BF)
+
+
+def _times(mask, block):
+    return (block.reshape(BS // TAIL, TAIL, BS) * mask[None]).reshape(BS, BS)
+
+
+def kernel(n_row, n_col, steps,
+           a_hbm, ai, ac, b_hbm, bi, bc, cm, out_ref,
+           abuf, bbuf, acc,
+           load_sem, a_send, a_recv, a_send2, a_recv2,
+           b_right, b_left, b_recv, b_send2, b_recv2):
+    r = lax.axis_index("row")
+    c = lax.axis_index("col")
+    d = lax.axis_index("depth")
+    sib = {"depth": 1 - d}
+    half = CB // 2
+
+    loads = []
+    for s in range(steps):
+        rows = pl.ds(s * BS, BS)
+        loads.append(pltpu.make_async_copy(b_hbm.at[0, 0, s, 0], bbuf.at[0, r, rows], load_sem.at[2 * s]))
+        loads.append(pltpu.make_async_copy(a_hbm.at[0, 0, s, 0], abuf.at[0, c, rows], load_sem.at[2 * s + 1]))
+    for load in loads:
+        load.start()
+
+    barrier = pltpu.get_barrier_semaphore()
+    pl.semaphore_signal(barrier, inc=1, device_id=sib)
+    for n in range(1, n_col):
+        pl.semaphore_signal(barrier, inc=1, device_id={"col": lax.rem(c + n, n_col)})
+
+    @pl.when(r > 0)
+    def _():
+        pl.semaphore_signal(barrier, inc=1, device_id={"row": r - 1})
+
+    @pl.when(r < n_row - 1)
+    def _():
+        pl.semaphore_signal(barrier, inc=1, device_id={"row": r + 1})
+
+    a_codes, b_codes = [], []
+    for s in range(steps):
+        a_codes.append(jnp.where(c < ac[0, d, s], ai[0, 0, s, 0], -1))
+        pos = bi[0, 0, s, 0]
+        b_codes.append(pos // CB)
+        b_codes.append(jnp.where(r < bc[0, d, s], pos % CB, -1))
+    abuf[0, c, pl.ds(steps * BS, TAIL)] = _rows(a_codes)
+    bbuf[0, r, pl.ds(steps * BS, TAIL)] = _rows(b_codes)
+
+    def b_copy(t, sems, target):
+        return pltpu.make_async_remote_copy(
+            src_ref=bbuf.at[0, t], dst_ref=bbuf.at[0, t], send_sem=sems.at[t], recv_sem=b_recv.at[t],
+            device_id={"row": target}, device_id_type=pl.DeviceIdType.MESH)
+
+    def b_across(t):
+        return pltpu.make_async_remote_copy(
+            src_ref=bbuf.at[0, t], dst_ref=bbuf.at[1, t], send_sem=b_send2.at[t], recv_sem=b_recv2.at[t],
+            device_id=sib, device_id_type=pl.DeviceIdType.MESH)
+
+    def a_copy(n, origin, target):
+        return pltpu.make_async_remote_copy(
+            src_ref=abuf.at[0, origin], dst_ref=abuf.at[0, origin], send_sem=a_send.at[n], recv_sem=a_recv.at[n],
+            device_id={"col": target}, device_id_type=pl.DeviceIdType.MESH)
+
+    def a_across(t):
+        return pltpu.make_async_remote_copy(
+            src_ref=abuf.at[0, t], dst_ref=abuf.at[1, t], send_sem=a_send2.at[t], recv_sem=a_recv2.at[t],
+            device_id=sib, device_id_type=pl.DeviceIdType.MESH)
+
+    pl.semaphore_wait(barrier, n_col + jnp.where(r > 0, 1, 0) + jnp.where(r < n_row - 1, 1, 0))
+    for load in loads:
+        load.wait()
+
+    @pl.when(r < n_row - 1)
+    def _():
+        b_copy(r, b_right, r + 1).start()
+
+    @pl.when(r > 0)
+    def _():
+        b_copy(r, b_left, r - 1).start()
+
+    for n in range(n_col - 1, 0, -1):
+        a_copy(n, c, c ^ n).start()
+    a_across(c).start()
+    b_across(r).start()
+
+    def pass_on(gap):
+        @pl.when(r >= gap)
+        def _():
+            t = r - gap
+            b_copy(t, b_right, r).wait_recv()
+
+            @pl.when(r < n_row - 1)
+            def _():
+                b_copy(t, b_right, r + 1).start()
+
+            b_across(t).start()
+
+        @pl.when(r + gap < n_row)
+        def _():
+            t = r + gap
+            b_copy(t, b_left, r).wait_recv()
+
+            @pl.when(r > 0)
+            def _():
+                b_copy(t, b_left, r - 1).start()
+
+            b_across(t).start()
+
+    def chunk(which, t, first):
+        b_tail = bbuf[which, t, pl.ds(steps * BS, TAIL)].astype(F32)
+        a_tails = [abuf[which, u, pl.ds(steps * BS, TAIL)].astype(F32) for u in range(n_col)]
+        xs, ys = [], []
+        for s in range(steps):
+            rows = pl.ds(s * BS, BS)
+            inner = jnp.broadcast_to(b_tail[2 * s:2 * s + 1], (TAIL, BS))
+            column = jnp.broadcast_to(b_tail[2 * s + 1:2 * s + 2], (TAIL, BS))
+            codes = [jnp.broadcast_to(tail[s:s + 1], (TAIL, BS)) - inner for tail in a_tails]
+            blocks = [abuf[which, u, rows] for u in range(n_col)]
+            parts = []
+            for i in range(RB):
+                total = None
+                for u in range(n_col):
+                    keep = jnp.where(codes[u] == float(i * PW), 1.0, 0.0).astype(BF)
+                    term = _times(keep, blocks[u])
+                    total = term if total is None else total + term
+                parts.append(total)
+            xs.append(jnp.concatenate(parts, axis=0))
+            block = bbuf[which, t, rows]
+            wanted = column - (d * half).astype(F32)
+            ys.append(jnp.concatenate(
+                [_times(jnp.where(wanted == float(j), 1.0, 0.0).astype(BF), block) for j in range(half)], axis=1))
+        x = jnp.concatenate(xs, axis=1)
+        y = jnp.concatenate(ys, axis=0)
+        product = jnp.dot(x, y, preferred_element_type=F32)
+        if first:
+            acc[...] = product
+        else:
+            acc[...] += product
+
+    pass_on(1)
+    for n in range(1, n_col):
+        a_copy(n, c, c ^ n).wait_recv()
+        a_across(c ^ n).start()
+    if n_row > 2:
+        pass_on(2)
+    chunk(0, r, True)
+    chunk(0, r ^ 1, False)
+    for gap in range(3, n_row):
+        pass_on(gap)
+    for n in range(2, n_row):
+        chunk(0, r ^ n, False)
+    for u in range(n_col):
+        a_across(u).wait_recv()
+    for n in range(n_row):
+        b_across(r ^ n).wait_recv()
+        chunk(1, r ^ n, False)
+
+    for i in range(RB):
+        for j in range(half):
+            keep = cm[i, j].astype(F32)
+            box = (pl.ds(i * BS, BS), pl.ds(j * BS, BS))
+            out_ref[box] = (acc[box] * keep).astype(BF)
+
+    for n in range(1, n_col):
+        a_copy(n, c, c ^ n).wait_send()
+    for u in range(n_col):
+        a_across(u).wait_send()
+    for t in range(n_row):
+        b_across(t).wait_send()
+
+        @pl.when((r >= t) & (r < n_row - 1))
+        def _():
+            b_copy(t, b_right, r).wait_send()
+
+        @pl.when((r <= t) & (r > 0))
+        def _():
+            b_copy(t, b_left, r).wait_send()
+
+
+def fused(n_row, n_col, *args):
+    a_blocks, b_blocks = args[0], args[3]
+    steps = a_blocks.shape[2]
+    smem = pl.BlockSpec(memory_space=pltpu.SMEM)
+    hbm = pl.BlockSpec(memory_space=pl.ANY)
+    rows = steps * BS + TAIL
+    dma = pltpu.SemaphoreType.DMA
+    return pl.pallas_call(
+        functools.partial(kernel, n_row, n_col, steps),
+        out_shape=jax.ShapeDtypeStruct((RB * BS, CB // 2 * BS), BF),
+        in_specs=[hbm, smem, smem, hbm, smem, smem, smem],
+        out_specs=pl.BlockSpec(memory_space=pltpu.VMEM),
+        scratch_shapes=[
+            pltpu.VMEM((2, n_col, rows, BS), BF),
+            pltpu.VMEM((2, n_row, rows, BS), BF),
+            pltpu.VMEM((RB * BS, CB // 2 * BS), F32),
+            dma((2 * steps,)),
+            dma((n_col,)), dma((n_col,)), dma((n_col,)), dma((n_col,)),
+            dma((n_row,)), dma((n_row,)), dma((n_row,)), dma((n_row,)), dma((n_row,)),
+        ],
+        compiler_params=pltpu.CompilerParams(
+            collective_id=0, has_side_effects=True, vmem_limit_bytes=32 * 2**20),
+    )(*args)
 
 
 def panel_term(a_blk, a_idx, a_cnt, b_blk, b_idx, b_cnt, col_start, col_count):
@@ -49,10 +264,11 @@
     return kept.reshape(RB * BS, half * BS).astype(jnp.bfloat16)
 
 
-def local(a_blocks, a_index, a_count, b_blocks, b_index, b_count, c_mask):
+def gathered(a_blocks, a_index, a_count, b_blocks, b_index, b_count, c_mask):
+    steps = a_blocks.shape[2]
     group = lax.axis_index("depth")
     total = jnp.zeros((RB * BS, CB * BS), jnp.float32)
-    for step in range(STEPS):
+    for step in range(steps):
         got_a, got_ai = (
             lax.all_gather(a_blocks[:, :, step : step + 1], "col", axis=3, tiled=True),
             lax.all_gather(a_index[:, :, step : step + 1], "col", axis=3, tiled=True),
@@ -78,6 +294,13 @@
 
 
 def solution(mesh):
+    n_row, n_col, n_depth = (mesh.shape[axis] for axis in ("row", "col", "depth"))
+
+    def local(*args):
+        one_slot_each = args[0].shape[3] == 1 and args[3].shape[3] == 1
+        short = n_depth == 2 and one_slot_each and n_row in (2, 4, 8) and n_col in (2, 4, 8)
+        return fused(n_row, n_col, *args) if short else gathered(*args)
+
     in_specs = (
         P("row", "depth", None, "col", None, None),
         P("row", "depth", None, "col"),

time: 106 us -> 23 us (0.22)
  blocking collectives: 59.9 us -> 0 us
  Pallas kernels: 0 us -> 18.1 us
  between operations: 13.6 us -> 0.02 us
  local copies, waits for them, and re-layouts: 14.4 us -> 4.67 us
  waiting for transfers between devices: 7.06 us -> 0 us
  matrix products: 6.35 us -> 0 us
  other arithmetic: 4.52 us -> 0 us
    all_gather x4 -> x0, blocking collectives: 44.1 us -> none  [the longest x2 26.7 us: local(): lax.all_gather(b_blocks[:, :, step:step + 1], 'row', axis=3, tiled=True)]
    pallas_call x0 -> x1, Pallas kernels: none -> 18.1 us  [fused(): pl.pallas_call(functools.partial(kernel, n_row, n_col, steps), out_shape=...]
    squeeze x1 -> x0, blocking collectives: 8.48 us -> none  [local(): got_bi[0, 0, 0]]
    unnamed x1 -> x0, blocking collectives: 7.35 us -> none
    reduce_scatter x1 -> x0, waiting for transfers between devices: 7.04 us -> none  [local(): lax.psum_scatter(total.astype(jnp.bfloat16), 'depth', scatter_dimension=1...]
    dot_general x8 -> x0, matrix products: 6.35 us -> none  [the longest x2 3.67 us: panel_term(): jnp.einsum('sn,sml->mnl', placer, products, precision=lax.Precision.HIGHE...]
    unnamed x15 -> x13, local copies, waits for them, and re-layouts: 9 us -> 4.67 us
    slice x4 -> x0, local copies, waits for them, and re-layouts: 3.51 us -> none  [the longest x1 1.38 us: local(): a_index[:, :, step:step + 1]]
  transfers between devices with their start and end apart: 1 -> 0, of which waited for: 1 -> 0; matrix products, arithmetic and copies ran while one was open for 0% -> 0% of each run, Pallas kernels for 0% -> 0%
where the time goes in v1:
time: 23 us; the launch traced here: 22.7 us
  Pallas kernels  18.1 us (79%)
  local copies, waits for them, and re-layouts  4.67 us (20%)
    pallas_call x1, Pallas kernels, fused(): pl.pallas_call(functools.partial(kernel, n_row, n_col, steps), out_shape=...  18.1 us
    unnamed x13, local copies, waits for them, and re-layouts  4.67 us

profile of v1, /device:TPU:0, one launch (start us, length us, event | category | flops | bytes accessed | tf_op | source)
XLA Modules:
  0.0 22.7 jit_solution(7541225942433778425)
XLA Ops:
  0.0 0.0 copy-start.2
  0.0 0.8 %copy.8.ai = s32[1,1,2,1]{3,2,1,0:T(2,128)S(1)} copy(s32[1,1,2,1]{2,3,1,0:T(1,128)} %param.8) | data formatting | bytes 16 | tf_op args[1]
  0.8 0.0 copy-start.3
  0.8 0.8 %copy.9.bi = s32[1,1,2,1]{3,2,1,0:T(2,128)S(1)} copy(s32[1,1,2,1]{2,3,1,0:T(1,128)} %param.11) | data formatting | bytes 16 | tf_op args[4]
  1.5 0.0 copy-done.2
  1.5 0.0 copy-done.3
  1.5 0.0 copy-start
  1.5 0.8 %copy-done = bf16[1,1,2,1,128,128]{5,4,3,2,1,0:T(8,128)(2,1)S(1)} copy-done((bf16[1,1,2,1,128,128]{5,4,3,2,1,0:T(8,128)(2,1)S(1)}, bf16[1,1,2,1,128,128]{5,4,3,2,1,0:T(8,128)(2,1)}, u32[]{:S(2)}) %copy-start) | copy-done | bytes 65560
  2.4 0.0 copy-start.1
  2.4 0.8 %copy-done.1 = bf16[1,1,2,1,128,128]{5,4,3,2,1,0:T(8,128)(2,1)S(1)} copy-done((bf16[1,1,2,1,128,128]{5,4,3,2,1,0:T(8,128)(2,1)S(1)}, bf16[1,1,2,1,128,128]{5,4,3,2,1,0:T(8,128)(2,1)}, u32[]{:S(2)}) %copy-start.1) | copy-done | bytes 65560
  3.2 0.0 copy-start.4
  3.2 0.7 %copy-done.4 = s32[1,2,2]{2,1,0:T(2,128)S(1)} copy-done((s32[1,2,2]{2,1,0:T(2,128)S(1)}, s32[1,2,2]{2,1,0:T(2,128)}, u32[]{:S(2)}) %copy-start.4) | copy-done | bytes 40
  3.9 18.1 %shard_map.73 = bf16[512,512]{1,0:T(8,128)(2,1)S(1)} custom-call(bf16[1,1,2,1,128,128]{5,4,3,2,1,0:T(8,128)(2,1)S(1)} %copy-done, s32[1,1,2,1]{3,2,1,0:T(2,128)S(1)} %copy.8.ai, s32[1,2,2]{2,1,0:T(2,128)S(1)} %copy-done.3, bf16[1,1,2,1,128,128]{5,4,3,2,1,0:T(8,128)(2,1)S(1)} %copy-done.1, s32[1,1,2,1]{3,2,1,0:T(2,128)S(1)} %copy.9.bi, ...), custom_call_target="tpu_custom_call" | custom-call | tf_op jit(solution)/shard_map/pallas_call | solution.py:210
  22.0 0.8 %copy.11 = bf16[512,512]{1,0:T(8,128)(2,1)} copy(bf16[512,512]{1,0:T(8,128)(2,1)S(1)} %shard_map.73) | data formatting | bytes 1048576
Async XLA Ops:
  0.0 1.5 %copy-start.2 = (s32[4,4]{1,0:T(4,128)S(1)}, s32[4,4]{1,0:T(4,128)}, u32[]{:S(2)}) copy-start(s32[4,4]{1,0:T(4,128)} %cm.1) | copy-start | bytes 196
  0.8 0.8 %copy-start.3 = (s32[1,2,2]{2,1,0:T(2,128)S(1)}, s32[1,2,2]{2,1,0:T(2,128)}, u32[]{:S(2)}) copy-start(s32[1,2,2]{2,1,0:T(2,128)} %ac.1) | copy-start | bytes 52
  1.5 0.8 %copy-start = (bf16[1,1,2,1,128,128]{5,4,3,2,1,0:T(8,128)(2,1)S(1)}, bf16[1,1,2,1,128,128]{5,4,3,2,1,0:T(8,128)(2,1)}, u32[]{:S(2)}) copy-start(bf16[1,1,2,1,128,128]{5,4,3,2,1,0:T(8,128)(2,1)} %a_hbm.1) | copy-start | bytes 196612
  2.4 0.8 %copy-start.1 = (bf16[1,1,2,1,128,128]{5,4,3,2,1,0:T(8,128)(2,1)S(1)}, bf16[1,1,2,1,128,128]{5,4,3,2,1,0:T(8,128)(2,1)}, u32[]{:S(2)}) copy-start(bf16[1,1,2,1,128,128]{5,4,3,2,1,0:T(8,128)(2,1)} %b_hbm.1) | copy-start | bytes 196612
  3.2 0.7 %copy-start.4 = (s32[1,2,2]{2,1,0:T(2,128)S(1)}, s32[1,2,2]{2,1,0:T(2,128)}, u32[]{:S(2)}) copy-start(s32[1,2,2]{2,1,0:T(2,128)} %bc.1) | copy-start | bytes 52

commit v2 on v0

--- a/solution.py
+++ b/solution.py
@@ -1,13 +1,206 @@
+import functools
+
 import jax
 import jax.numpy as jnp
 from jax import lax
+from jax.experimental import pallas as pl
+from jax.experimental.pallas import tpu as pltpu
 from jax.sharding import PartitionSpec as P
 
 BS = 128
 PW = 8
-STEPS = 2
 RB = 4
 CB = 8
+TAIL = 16
+BF = jnp.bfloat16
+F32 = jnp.float32
+
+
+def _rows(values):
+    row = lax.broadcasted_iota(jnp.int32, (TAIL, BS), 0)
+    tile = jnp.zeros((TAIL, BS), jnp.int32)
+    for r, value in enumerate(values):
+        tile = jnp.where(row == r, value, tile)
+    return tile.astype(F32).astype(BF)
+
+
+def _times(mask, block):
+    return (block.reshape(BS // TAIL, TAIL, BS) * mask[None]).reshape(BS, BS)
+
+
+def kernel(n_row, n_col, steps,
+           a_hbm, ai_hbm, ac_hbm, b_hbm, bi_hbm, bc_hbm, cm_hbm, out_ref,
+           abuf, bbuf, acc, ai, ac, bi, bc, cm,
+           load_sem, small_sem, a_send, a_recv, a_send2, a_recv2,
+           b_send, b_recv, b_send2, b_recv2):
+    r = lax.axis_index("row")
+    c = lax.axis_index("col")
+    d = lax.axis_index("depth")
+    sib = {"depth": 1 - d}
+    half = CB // 2
+
+    small = [pltpu.make_async_copy(src, dst, small_sem.at[n]) for n, (src, dst) in enumerate(
+        [(ai_hbm, ai), (ac_hbm, ac), (bi_hbm, bi), (bc_hbm, bc), (cm_hbm, cm)])]
+    for load in small:
+        load.start()
+    loads = []
+    for s in range(steps):
+        rows = pl.ds(TAIL + s * BS, BS)
+        loads.append(pltpu.make_async_copy(b_hbm.at[0, 0, s, 0], bbuf.at[0, r, rows], load_sem.at[2 * s]))
+        loads.append(pltpu.make_async_copy(a_hbm.at[0, 0, s, 0], abuf.at[0, c, rows], load_sem.at[2 * s + 1]))
+    for load in loads:
+        load.start()
+
+    barrier = pltpu.get_barrier_semaphore()
+    pl.semaphore_signal(barrier, inc=1, device_id=sib)
+    for n in range(1, n_col):
+        pl.semaphore_signal(barrier, inc=1, device_id={"col": lax.rem(c + n, n_col)})
+
+    for n in range(1, n_row):
+        pl.semaphore_signal(barrier, inc=1, device_id={"row": r ^ n})
+
+    for load in small:
+        load.wait()
+    a_codes, b_codes = [], []
+    for s in range(steps):
+        a_codes.append(jnp.where(c < ac[d, s], ai[0, s], -1))
+        pos = bi[0, s]
+        b_codes.append(pos // CB)
+        b_codes.append(jnp.where(r < bc[d, s], pos % CB, -1))
+    abuf[0, c, pl.ds(0, TAIL)] = _rows(a_codes)
+    bbuf[0, r, pl.ds(0, TAIL)] = _rows(b_codes)
+
+    pieces = [pl.ds(0, TAIL + BS)] + [pl.ds(TAIL + s * BS, BS) for s in range(1, steps)]
+
+    def remote(src, dst, send, recv, target):
+        return pltpu.make_async_remote_copy(
+            src_ref=src, dst_ref=dst, send_sem=send, recv_sem=recv,
+            device_id=target, device_id_type=pl.DeviceIdType.MESH)
+
+    def b_copy(n, p, origin, target):
+        ref = bbuf.at[0, origin, pieces[p]]
+        return remote(ref, ref, b_send.at[n, p], b_recv.at[n, p], {"row": target})
+
+    def b_across(t, p):
+        return remote(bbuf.at[0, t, pieces[p]], bbuf.at[1, t, pieces[p]], b_send2.at[t, p], b_recv2.at[t, p], sib)
+
+    def a_copy(n, p, origin, target):
+        ref = abuf.at[0, origin, pieces[p]]
+        return remote(ref, ref, a_send.at[n, p], a_recv.at[n, p], {"col": target})
+
+    def a_across(t, p):
+        return remote(abuf.at[0, t, pieces[p]], abuf.at[1, t, pieces[p]], a_send2.at[t, p], a_recv2.at[t, p], sib)
+
+    pl.semaphore_wait(barrier, n_col + n_row - 1)
+    for load in loads:
+        load.wait()
+
+    for p in range(steps):
+        for n in range(1, n_row):
+            b_copy(n, p, r, r ^ n).start()
+        for n in range(n_col - 1, 0, -1):
+            a_copy(n, p, c, c ^ n).start()
+    for p in range(steps):
+        b_across(r, p).start()
+        a_across(c, p).start()
+
+    def factors(which, t):
+        b_tail = bbuf[which, t, pl.ds(0, TAIL)].astype(F32)
+        a_tails = [abuf[which, u, pl.ds(0, TAIL)].astype(F32) for u in range(n_col)]
+        xs, ys = [], []
+        for s in range(steps):
+            rows = pl.ds(TAIL + s * BS, BS)
+            inner = jnp.broadcast_to(b_tail[2 * s:2 * s + 1], (TAIL, BS))
+            column = jnp.broadcast_to(b_tail[2 * s + 1:2 * s + 2], (TAIL, BS))
+            codes = [jnp.broadcast_to(tail[s:s + 1], (TAIL, BS)) - inner for tail in a_tails]
+            blocks = [abuf[which, u, rows] for u in range(n_col)]
+            parts = []
+            for i in range(RB):
+                total = None
+                for u in range(n_col):
+                    keep = jnp.where(codes[u] == float(i * PW), 1.0, 0.0).astype(BF)
+                    term = _times(keep, blocks[u])
+                    total = term if total is None else total + term
+                parts.append(total)
+            xs.append(jnp.concatenate(parts, axis=0))
+            block = bbuf[which, t, rows]
+            wanted = column - (d * half).astype(F32)
+            ys.append(jnp.concatenate(
+                [_times(jnp.where(wanted == float(j), 1.0, 0.0).astype(BF), block) for j in range(half)], axis=1))
+        return xs, ys
+
+    def stage(t, first):
+        mine, other = factors(0, t), factors(1, t)
+        x = jnp.concatenate(mine[0] + other[0], axis=1)
+        y = jnp.concatenate(mine[1] + other[1], axis=0)
+        product = jnp.dot(x, y, preferred_element_type=F32)
+        if first:
+            acc[...] = product
+        else:
+            acc[...] += product
+
+    for p in range(steps):
+        for n in range(1, n_col):
+            a_copy(n, p, c, c ^ n).wait_recv()
+            a_across(c ^ n, p).start()
+    for n in range(1, n_row):
+        for p in range(steps):
+            b_copy(n, p, r, r ^ n).wait_recv()
+            b_across(r ^ n, p).start()
+    for u in range(n_col):
+        for p in range(steps):
+            a_across(u, p).wait_recv()
+    for n in range(n_row):
+        for p in range(steps):
+            b_across(r ^ n, p).wait_recv()
+        stage(r ^ n, n == 0)
+
+    for i in range(RB):
+        for j in range(half):
+            keep = cm[i, j].astype(F32)
+            box = (pl.ds(i * BS, BS), pl.ds(j * BS, BS))
+            out_ref[box] = (acc[box] * keep).astype(BF)
+
+    for p in range(steps):
+        for n in range(1, n_col):
+            a_copy(n, p, c, c ^ n).wait_send()
+        for u in range(n_col):
+            a_across(u, p).wait_send()
+        for n in range(1, n_row):
+            b_copy(n, p, r, r ^ n).wait_send()
+        for t in range(n_row):
+            b_across(t, p).wait_send()
+
+
+def fused(n_row, n_col, *args):
+    a_blocks, a_index, a_count, b_blocks, b_index, b_count, c_mask = args
+    steps = a_blocks.shape[2]
+    args = (a_blocks, a_index.reshape(1, steps), a_count.reshape(a_count.shape[1:]),
+            b_blocks, b_index.reshape(1, steps), b_count.reshape(b_count.shape[1:]), c_mask)
+    hbm = pl.BlockSpec(memory_space=pltpu.HBM)
+    rows = steps * BS + TAIL
+    dma = pltpu.SemaphoreType.DMA
+    return pl.pallas_call(
+        functools.partial(kernel, n_row, n_col, steps),
+        out_shape=jax.ShapeDtypeStruct((RB * BS, CB // 2 * BS), BF),
+        in_specs=[hbm] * 7,
+        out_specs=pl.BlockSpec(memory_space=pltpu.VMEM),
+        scratch_shapes=[
+            pltpu.VMEM((2, n_col, rows, BS), BF),
+            pltpu.VMEM((2, n_row, rows, BS), BF),
+            pltpu.VMEM((RB * BS, CB // 2 * BS), F32),
+            pltpu.SMEM((1, steps), jnp.int32),
+            pltpu.SMEM((2, steps), jnp.int32),
+            pltpu.SMEM((1, steps), jnp.int32),
+            pltpu.SMEM((2, steps), jnp.int32),
+            pltpu.SMEM(c_mask.shape, jnp.int32),
+            dma((2 * steps,)), dma((5,)),
+            dma((n_col, steps)), dma((n_col, steps)), dma((n_col, steps)), dma((n_col, steps)),
+            dma((n_row, steps)), dma((n_row, steps)), dma((n_row, steps)), dma((n_row, steps)),
+        ],
+        compiler_params=pltpu.CompilerParams(
+            collective_id=0, has_side_effects=True, vmem_limit_bytes=63 * 2**20),
+    )(*args)
 
 
 def panel_term(a_blk, a_idx, a_cnt, b_blk, b_idx, b_cnt, col_start, col_count):
@@ -49,10 +242,11 @@
     return kept.reshape(RB * BS, half * BS).astype(jnp.bfloat16)
 
 
-def local(a_blocks, a_index, a_count, b_blocks, b_index, b_count, c_mask):
+def gathered(a_blocks, a_index, a_count, b_blocks, b_index, b_count, c_mask):
+    steps = a_blocks.shape[2]
     group = lax.axis_index("depth")
     total = jnp.zeros((RB * BS, CB * BS), jnp.float32)
-    for step in range(STEPS):
+    for step in range(steps):
         got_a, got_ai = (
             lax.all_gather(a_blocks[:, :, step : step + 1], "col", axis=3, tiled=True),
             lax.all_gather(a_index[:, :, step : step + 1], "col", axis=3, tiled=True),
@@ -78,6 +272,13 @@
 
 
 def solution(mesh):
+    n_row, n_col, n_depth = (mesh.shape[axis] for axis in ("row", "col", "depth"))
+
+    def local(*args):
+        one_slot_each = args[0].shape[3] == 1 and args[3].shape[3] == 1
+        short = n_depth == 2 and one_slot_each and n_row in (2, 4, 8) and n_col in (2, 4, 8)
+        return fused(n_row, n_col, *args) if short else gathered(*args)
+
     in_specs = (
         P("row", "depth", None, "col", None, None),
         P("row", "depth", None, "col"),

time: 106 us -> 17.8 us (0.17)
  blocking collectives: 59.9 us -> 0 us
  Pallas kernels: 0 us -> 15.7 us
  between operations: 13.6 us -> 0.01 us
  local copies, waits for them, and re-layouts: 14.4 us -> 1.87 us
  waiting for transfers between devices: 7.06 us -> 0 us
  matrix products: 6.35 us -> 0 us
  other arithmetic: 4.52 us -> 0 us
    all_gather x4 -> x0, blocking collectives: 44.1 us -> none  [the longest x2 26.7 us: local(): lax.all_gather(b_blocks[:, :, step:step + 1], 'row', axis=3, tiled=True)]
    pallas_call x0 -> x1, Pallas kernels: none -> 15.7 us  [fused(): pl.pallas_call(functools.partial(kernel, n_row, n_col, steps), out_shape=...]
    squeeze x1 -> x0, blocking collectives: 8.48 us -> none  [local(): got_bi[0, 0, 0]]
    unnamed x1 -> x0, blocking collectives: 7.35 us -> none
    unnamed x15 -> x1, local copies, waits for them, and re-layouts: 9 us -> 1.87 us
    reduce_scatter x1 -> x0, waiting for transfers between devices: 7.04 us -> none  [local(): lax.psum_scatter(total.astype(jnp.bfloat16), 'depth', scatter_dimension=1...]
    dot_general x8 -> x0, matrix products: 6.35 us -> none  [the longest x2 3.67 us: panel_term(): jnp.einsum('sn,sml->mnl', placer, products, precision=lax.Precision.HIGHE...]
    slice x4 -> x0, local copies, waits for them, and re-layouts: 3.51 us -> none  [the longest x1 1.38 us: local(): a_index[:, :, step:step + 1]]
  transfers between devices with their start and end apart: 1 -> 0, of which waited for: 1 -> 0; matrix products, arithmetic and copies ran while one was open for 0% -> 0% of each run, Pallas kernels for 0% -> 0%
where the time goes in v2:
time: 17.8 us; the launch traced here: 17.6 us
  Pallas kernels  15.7 us (88%)
  local copies, waits for them, and re-layouts  1.87 us (11%)
    pallas_call x1, Pallas kernels, fused(): pl.pallas_call(functools.partial(kernel, n_row, n_col, steps), out_shape=...  15.7 us
    unnamed x1, local copies, waits for them, and re-layouts  1.87 us

profile of v2, /device:TPU:0, one launch (start us, length us, event | category | flops | bytes accessed | tf_op | source)
XLA Modules:
  0.0 17.6 jit_solution(52945421950463549)
XLA Ops:
  0.0 15.7 %shard_map.73 = bf16[512,512]{1,0:T(8,128)(2,1)} custom-call(bf16[1,1,2,1,128,128]{5,4,3,2,1,0:T(8,128)(2,1)} %a_hbm.1, s32[1,2]{1,0:T(1,128)} %bitcast.6, s32[2,2]{1,0:T(2,128)} %bitcast.4, bf16[1,1,2,1,128,128]{5,4,3,2,1,0:T(8,128)(2,1)} %b_hbm.1, s32[1,2]{1,0:T(1,128)} %bitcast.7, s32[2,2]{1,0:T(2,128)} %bitcast.5, s32[4,4]{1,0:T(4,128)} %cm_hbm.1), custom_call_target="tpu_custom_call" | custom-call | tf_op jit(solution)/shard_map/pallas_call | solution.py:183
  15.7 1.9 %copy.9 = bf16[512,512]{1,0:T(8,128)(2,1)} copy(bf16[512,512]{1,0:T(8,128)(2,1)} %shard_map.73) | data formatting | bytes 1048576

commit v3 on v2

--- a/solution.py
+++ b/solution.py
@@ -177,6 +177,7 @@
     steps = a_blocks.shape[2]
     args = (a_blocks, a_index.reshape(1, steps), a_count.reshape(a_count.shape[1:]),
             b_blocks, b_index.reshape(1, steps), b_count.reshape(b_count.shape[1:]), c_mask)
+    args = tuple(pltpu.with_memory_space_constraint(arg, pltpu.HBM) for arg in args)
     hbm = pl.BlockSpec(memory_space=pltpu.HBM)
     rows = steps * BS + TAIL
     dma = pltpu.SemaphoreType.DMA
@@ -199,7 +200,7 @@
             dma((n_row, steps)), dma((n_row, steps)), dma((n_row, steps)), dma((n_row, steps)),
         ],
         compiler_params=pltpu.CompilerParams(
-            collective_id=0, has_side_effects=True, vmem_limit_bytes=63 * 2**20),
+            collective_id=0, has_side_effects=True, vmem_limit_bytes=32 * 2**20),
     )(*args)
 
 

time: 17.8 us -> 15.9 us (0.89)
  local copies, waits for them, and re-layouts: 1.87 us -> 0.8 us
  Pallas kernels: 15.7 us -> 14.9 us
    unnamed x1, local copies, waits for them, and re-layouts: 1.87 us -> 0.8 us
    pallas_call x1, Pallas kernels: 15.7 us -> 14.9 us  [fused(): pl.pallas_call(functools.partial(kernel, n_row, n_col, steps), out_shape=...]
where the time goes in v3:
time: 15.9 us; the launch traced here: 15.7 us
  Pallas kernels  14.9 us (94%)
  local copies, waits for them, and re-layouts  0.8 us (5%)
    pallas_call x1, Pallas kernels, fused(): pl.pallas_call(functools.partial(kernel, n_row, n_col, steps), out_shape=...  14.9 us
    unnamed x1, local copies, waits for them, and re-layouts  0.8 us

profile of v3, /device:TPU:0, one launch (start us, length us, event | category | flops | bytes accessed | tf_op | source)
XLA Modules:
  0.0 15.7 jit_solution(1032189781024326817)
XLA Ops:
  0.0 14.9 %shard_map.73 = bf16[512,512]{1,0:T(8,128)(2,1)S(1)} custom-call(bf16[1,1,2,1,128,128]{5,4,3,2,1,0:T(8,128)(2,1)} %a_hbm.1, s32[1,2]{1,0:T(1,128)} %bitcast.6, s32[2,2]{1,0:T(2,128)} %bitcast.4, bf16[1,1,2,1,128,128]{5,4,3,2,1,0:T(8,128)(2,1)} %b_hbm.1, s32[1,2]{1,0:T(1,128)} %bitcast.7, s32[2,2]{1,0:T(2,128)} %bitcast.5, s32[4,4]{1,0:T(4,128)} %cm_hbm.1), custom_call_target="tpu_custom_call" | custom-call | tf_op jit(solution)/shard_map/pallas_call | solution.py:184
  14.9 0.8 %copy.9 = bf16[512,512]{1,0:T(8,128)(2,1)} copy(bf16[512,512]{1,0:T(8,128)(2,1)S(1)} %shard_map.73) | data formatting | bytes 1048576
